TPU v7x, 32 devices: a whole 2x2x4 slice. The times are simulated.
32 devices in a mesh: mesh: 4 (over y, core), mode: 8 (over z, x).
Axes of the slice: x: 2, y: 2, z: 4, core: 2. Of those that a mesh axis runs over, the one named last changes fastest.
Arguments:
- field: float32 [256, 512, 1024], P('mode', 'mesh'), may hold values from -6 to 6
- kappa: bfloat16 [3, 512, 1024], P(None, ('mesh', 'mode')), may hold values from 0.099609375 to 1
- mass: float32 [512, 1024], P(('mesh', 'mode')), may hold values from 0.5 to 1.5
- kl_modes: bfloat16 [3, 256, 256], replicated, may hold values from -0.375 to 0.375
- to_points: bfloat16 [512, 256], replicated, may hold values from -0.375 to 0.375
- from_points: bfloat16 [256, 512], replicated, may hold values from -0.25 to 0.25
- capacity: float32 [512], replicated, may hold values from 0.5 to 2
- latent: float32 [512], replicated, may hold values from 0.5 to 3
Outputs:
- residual: bfloat16 [256, 512, 1024], P('mode', 'mesh')
All inputs are finite; a program needn't handle non-finite values.
Results may differ from a plain program's by a relative error of at most 0.0058.
Values may be sent and summed in bfloat16 or wider, within the bound.
A program may use at most 256 MiB of HBM per device.

v0:
```python
import jax
import jax.numpy as jnp
from jax import lax
from jax.sharding import PartitionSpec as P


def extended(cells, sides, width):
    for axis, dim in sides:
        count = lax.axis_size(axis)
        ends = count - 1
        head = lax.slice_in_dim(cells, 0, width, axis=dim)
        tail = lax.slice_in_dim(cells, cells.shape[dim] - width, cells.shape[dim], axis=dim)
        cells = jnp.concatenate(
            [
                lax.ppermute(tail, axis, [(i, (i + 1) % count) for i in range(ends)]),
                cells,
                lax.ppermute(head, axis, [((i + 1) % count, i) for i in range(ends)]),
            ],
            axis=dim,
        )
    return cells


def conduct(values, kappa):
    count = values.shape[1] - 2
    width = values.shape[2]
    vals = jnp.pad(values.astype(jnp.float32), ((0, 0), (0, 0), (1, 1)))[None]
    kaps = jnp.pad(kappa.astype(jnp.float32), ((0, 0), (0, 0), (1, 1)))[:, None]
    centre = vals[:, :, 1 : 1 + count, 1 : 1 + width]
    kcentre = kaps[:, :, 1 : 1 + count, 1 : 1 + width]
    total = jnp.zeros((kaps.shape[0], vals.shape[1], count, width), jnp.float32)
    for shift_x, shift_y in ((0, 1), (2, 1), (1, 0), (1, 2)):
        other = vals[:, :, shift_x : shift_x + count, shift_y : shift_y + width]
        kother = kaps[:, :, shift_x : shift_x + count, shift_y : shift_y + width]
        total = total + 0.5 * (kcentre + kother) * (centre - other)
    return total.astype(jnp.bfloat16)


def finish(coarse, images, mass_rows, kl_modes, to_points, from_points, capacity, latent):
    mixed = jnp.einsum("kij,kjxy->ixy", kl_modes, images, preferred_element_type=jnp.float32)
    temps = jnp.einsum("qi,ixy->qxy", to_points, coarse, preferred_element_type=jnp.float32)
    heat = (
        capacity[:, None, None] * temps + latent[:, None, None] * jax.nn.sigmoid(2.0 * temps)
    ).astype(jnp.bfloat16)
    enthalpy = jnp.einsum("iq,qxy->ixy", from_points, heat, preferred_element_type=jnp.float32)
    return (mass_rows[None] * enthalpy + mixed).astype(jnp.bfloat16)


def body(field, kappa, mass, kl_modes, to_points, from_points, capacity, latent):
    coarse = field.astype(jnp.bfloat16)
    owned = coarse.shape[0]
    width = coarse.shape[2]
    groups = lax.axis_size("mode")
    terms = kappa.shape[0]
    kap_rows = lax.all_gather(kappa, "mode", axis=1, tiled=True)
    stacked = jnp.concatenate([coarse, kap_rows], 0)
    padded = extended(stacked, (("mesh", 1),), 1)
    images = conduct(padded[:owned], padded[owned:])
    joined = jnp.concatenate([coarse[None], images], 0)
    joined = joined.reshape((terms + 1) * owned, coarse.shape[1], width)
    moved = lax.all_to_all(joined, "mode", split_axis=1, concat_axis=0, tiled=True)
    node_rows = moved.shape[1]
    moved = moved.reshape(groups, terms + 1, owned, node_rows, width)
    moved = jnp.transpose(moved, (1, 0, 2, 3, 4)).reshape(
        terms + 1, groups * owned, node_rows, width
    )
    node_coarse = moved[0]
    node_images = moved[1:]
    result = finish(
        node_coarse, node_images, mass, kl_modes, to_points, from_points, capacity, latent
    )
    return lax.all_to_all(result, "mode", split_axis=0, concat_axis=1, tiled=True)


def solution(mesh):
    in_specs = (
        P("mode", "mesh", None),
        P(None, ("mesh", "mode"), None),
        P(("mesh", "mode"), None),
        P(),
        P(),
        P(),
        P(),
        P(),
    )
    out_specs = P("mode", "mesh", None)
    return jax.shard_map(body, mesh=mesh, in_specs=in_specs, out_specs=out_specs, check_vma=False)
```

profile of v0, /device:TPU:1, one launch (start us, length us, event | category | flops | bytes accessed | tf_op | source)
XLA Modules:
  0.0 1315.9 jit_solution(11272950333644281777)
XLA Ops:
  0.0 0.0 copy-start
  0.0 0.0 slice-start
  0.0 0.0 slice-start.1
  0.0 0.0 slice-start.2
  0.0 0.0 copy-start.2
  0.0 16.5 %copy.54 = bf16[32,128,1024]{2,0,1:T(8,128)(2,1)S(1)} copy(f32[32,128,1024]{2,1,0:T(8,128)} %param.8) | data formatting | bytes 25165824 | tf_op args[0]
  16.6 0.0 copy-done.2
  16.6 0.0 copy-start.1
  16.6 28.1 %all_gather.3 = bf16[3,128,1024]{2,1,0:T(8,128)(2,1)S(1)} all-gather(bf16[3,16,1024]{2,1,0:T(8,128)(2,1)S(1)} %copy-done.2), channel_id=1, replica_groups=mesh['mesh'=4,'mode'=8] {'mode'}, dimensions={1}, use_global_device_ids=true | all-gather | bytes 884736 | tf_op jit(solution)/shard_map/all_gather | solution.py:55
  44.6 0.7 copy.32
  45.3 0.0 slice-start.3
  45.4 9.1 collective-permute-start
  54.5 2.1 collective-permute-start.1
  56.7 0.0 slice-done
  56.7 0.0 slice-done.1
  56.7 0.0 slice-done.2
  56.7 0.0 slice-done.3
  56.7 11.4 copy.56
  68.1 0.0 collective-permute-done
  68.1 0.0 collective-permute-done.1
  68.1 0.0 copy-done.1
  68.1 12.0 fusion.11
  80.1 51.1 %fusion.6 = (f32[32,128,1024]{2,0,1:T(8,128)}, f32[32,128,1024]{2,0,1:T(8,128)}, f32[32,128,1024]{2,0,1:T(8,128)}, f32[32,128,1024]{2,0,1:T(8,128)}) fusion(f32[1,32,130,1026]{3,1,2,0:T(8,128)} %fusion.11), kind=kLoop, calls=%fused_computation.15 | loop fusion | flops 16777216 | bytes 150994944 | tf_op jit(solution)/shard_map/mul | solution.py:35
  131.2 0.0 slice-start.4
  131.2 0.0 slice-start.5
  131.2 2.9 fusion.38
  134.1 0.0 slice-start.6
  134.1 0.0 slice-start.7
  134.1 4.5 fusion.36
  138.6 0.0 slice-done.4
  138.6 0.0 slice-done.5
  138.7 0.0 slice-done.6
  138.7 0.0 slice-done.7
  138.7 46.6 %add_convert_fusion = bf16[3,32,128,1024]{3,1,0,2:T(8,128)(2,1)} fusion(f32[32,128,1024]{2,0,1:T(8,128)} %get-tuple-element.8, f32[3,128,1024]{2,0,1:T(4,128)S(1)} %get-tuple-element.14, f32[32,128,1024]{2,0,1:T(8,128)} %get-tuple-element.6, f32[3,128,1024]{2,0,1:T(4,128)S(1)} %get-tuple-element.12, f32[32,128,1024]{2,0,1:T(8,128)} %get-tuple-element.7, ...), kind=kLoop, calls=%fused_computation | loop fusion | flops 100663296 | bytes 98566144 | tf_op jit(solution)/shard_map/convert_element_type | solution.py:36
  185.3 23.1 %pad_maximum_fusion = bf16[4,32,128,1024]{3,1,0,2:T(8,128)(2,1)} fusion(bf16[3,32,128,1024]{3,1,0,2:T(8,128)(2,1)} %add_convert_fusion, bf16[1,32,128,1024]{3,1,0,2:T(8,128)(2,1)} %bitcast.79), kind=kLoop, calls=%fused_computation.1 | loop fusion | flops 16777216 | bytes 67108864 | tf_op jit(solution)/shard_map/concatenate | solution.py:59
  208.4 733.1 %all_to_all.33 = bf16[128,128,1024]{2,0,1:T(8,128)(2,1)} all-to-all(bf16[128,128,1024]{2,0,1:T(8,128)(2,1)} %bitcast.72), channel_id=1, replica_groups=mesh['mesh'=4,'mode'=8] {'mode'}, dimensions={1} | all-to-all | bytes 67108864 | tf_op jit(solution)/shard_map/all_to_all | solution.py:61
  941.5 30.8 %copy.35 = bf16[8,128,16,1024]{3,2,1,0:T(8,128)(2,1)} copy(bf16[8,128,16,1024]{3,1,2,0:T(8,128)(2,1)} %bitcast.73) | data formatting | bytes 67108864 | tf_op jit(solution)/shard_map/all_to_all | solution.py:61
  972.3 21.4 %slice.80 = bf16[3,8,32,16,1024]{4,3,2,0,1:T(8,128)(2,1)} slice(bf16[4,8,32,16,1024]{4,3,2,0,1:T(8,128)(2,1)} %bitcast.70), slice={[1:4], [0:8], [0:32], [0:16], [0:1024]} | slice | bytes 50331648 | tf_op jit(solution)/shard_map/slice | solution.py:68
  993.7 8.7 slice.79
  1002.4 21.3 %copy.37 = bf16[3,8,32,16,1024]{4,3,2,1,0:T(8,128)(2,1)} copy(bf16[3,8,32,16,1024]{4,3,2,0,1:T(8,128)(2,1)} %slice.80) | data formatting | bytes 50331648 | tf_op jit(solution)/shard_map/slice | solution.py:68
  1023.7 0.0 copy-done
  1023.7 0.0 copy-start.3
  1023.7 0.0 copy-start.4
  1023.7 0.0 copy-start.5
  1023.8 0.0 copy-start.6
  1023.8 0.0 copy-start.7
  1023.8 59.9 %fusion = f32[16,1024,256,1]{2,1,3,0:T(8,128)} fusion(bf16[3,256,16,1024]{3,2,1,0:T(8,128)(2,1)} %bitcast.80, bf16[3,256,256]{2,1,0:T(8,128)(2,1)S(1)} %copy-done), kind=kOutput, calls=%fused_computation.5 | convolution fusion | flops 6442450944 | bytes 42336256 | tf_op jit(solution)/shard_map/kij,kjxy->ixy/dot_general | solution.py:40
  1083.7 0.0 copy-done.3
  1083.7 0.0 copy-done.4
  1083.7 0.0 copy-done.5
  1083.8 0.0 copy-done.6
  1083.8 0.0 copy-done.7
  1083.8 22.9 %fusion.23 = bf16[256,16,1024]{0,2,1:T(8,128)(2,1)} fusion(f32[16,1024,256,1]{2,1,3,0:T(8,128)} %fusion, f32[512]{0:T(512)S(1)} %copy-done.6, f32[512]{0:T(512)S(1)} %copy-done.7, bf16[256,16,1024]{2,1,0:T(8,128)(2,1)} %bitcast.81, f32[16,1024]{1,0:T(8,128)S(1)} %copy-done.5, bf16[256,512]{1,0:T(8,128)(2,1)S(1)} %copy-done.3, bf16[512,256]{1,0:T(8,128)(2,1)S(1)} %copy-done.4), kind=kOutput, calls=%fused_computation.30 | convolution fusion | flops 8669626368 | bytes 34148352 | tf_op jit(solution)/shard_map/iq,qxy->ixy/dot_general | solution.py:45
  1106.6 12.2 copy.39
  1118.9 187.9 %all_to_all.34 = bf16[256,16,1024]{2,1,0:T(8,128)(2,1)} all-to-all(bf16[256,16,1024]{2,1,0:T(8,128)(2,1)} %copy.39), channel_id=1, replica_groups=mesh['mesh'=4,'mode'=8] {'mode'}, dimensions={0} | all-to-all | bytes 16777216 | tf_op jit(solution)/shard_map/all_to_all | solution.py:72
  1306.8 8.7 copy.40
  (3 shorter events, 0.0 us)
Async XLA Ops:
  0.0 1023.7 %copy-start = (bf16[3,256,256]{2,1,0:T(8,128)(2,1)S(1)}, bf16[3,256,256]{2,1,0:T(8,128)(2,1)}, u32[]{:S(2)}) copy-start(bf16[3,256,256]{2,1,0:T(8,128)(2,1)} %param.11) | copy-start | bytes 1179652
  0.0 56.6 %slice-start = ((s8[16777216]{0:T(1024)(128)(4,1)}), s8[4194304]{0:T(1024)(128)(4,1)S(1)}, s32[]{:S(2)}) async-start(s8[16777216]{0:T(1024)(128)(4,1)} %bitcast.74), calls=%async_computation.2 | async-start | bytes 8388608
  0.0 56.7 %slice-start.1 = ((s8[16777216]{0:T(1024)(128)(4,1)}), s8[4194304]{0:T(1024)(128)(4,1)S(1)}, s32[]{:S(2)}) async-start(s8[16777216]{0:T(1024)(128)(4,1)} %bitcast.74), calls=%async_computation.3 | async-start | bytes 8388608
  0.0 56.7 %slice-start.2 = ((s8[16777216]{0:T(1024)(128)(4,1)}), s8[4194304]{0:T(1024)(128)(4,1)S(1)}, s32[]{:S(2)}) async-start(s8[16777216]{0:T(1024)(128)(4,1)} %bitcast.74), calls=%async_computation.4 | async-start | bytes 8388608
  0.0 16.6 %copy-start.2 = (bf16[3,16,1024]{2,1,0:T(8,128)(2,1)S(1)}, bf16[3,16,1024]{2,1,0:T(8,128)(2,1)}, u32[]{:S(2)}) copy-start(bf16[3,16,1024]{2,1,0:T(8,128)(2,1)} %param.9) | copy-start | bytes 294916
  16.6 51.5 %copy-start.1 = (bf16[32,128,1024]{2,0,1:T(8,128)(2,1)}, bf16[32,128,1024]{2,0,1:T(8,128)(2,1)S(1)}, u32[]{:S(2)}) copy-start(bf16[32,128,1024]{2,0,1:T(8,128)(2,1)S(1)} %copy.54) | copy-start | bytes 25165828
  45.3 11.4 slice-start.3
  45.4 22.8 %collective-permute-start = (bf16[35,1,1024]{2,0,1:T(8,128)(2,1)S(1)}, bf16[35,1,1024]{2,0,1:T(8,128)(2,1)S(1)}, u32[]{:S(2)}, u32[]{:S(2)}) collective-permute-start(bf16[35,1,1024]{2,0,1:T(8,128)(2,1)S(1)} %get-tuple-element.9), channel_id=1, source_target_pairs={{0,8},{8,16},{16,24},{1,9},{9,17},{17,25},{2,10},{10,18},{18,26},{... | collective-permute-start | bytes 215048 | tf_op jit(solution)/shard_map/ppermute | solution.py:15
  54.5 13.6 %collective-permute-start.1 = (bf16[35,1,1024]{2,0,1:T(8,128)(2,1)S(1)}, bf16[35,1,1024]{2,0,1:T(8,128)(2,1)S(1)}, u32[]{:S(2)}, u32[]{:S(2)}) collective-permute-start(bf16[35,1,1024]{2,0,1:T(8,128)(2,1)S(1)} %get-tuple-element.10), channel_id=1, source_target_pairs={{8,0},{16,8},{24,16},{9,1},{17,9},{25,17},{10,2},{18,10},{26,18},{... | collective-permute-start | bytes 215048 | tf_op jit(solution)/shard_map/ppermute | solution.py:17
  131.2 7.5 slice-start.4
  131.2 7.5 slice-start.5
  134.1 4.6 slice-start.6
  134.1 4.6 slice-start.7
  1023.7 60.0 %copy-start.3 = (bf16[256,512]{1,0:T(8,128)(2,1)S(1)}, bf16[256,512]{1,0:T(8,128)(2,1)}, u32[]{:S(2)}) copy-start(bf16[256,512]{1,0:T(8,128)(2,1)} %param.13) | copy-start | bytes 786436
  1023.7 60.0 %copy-start.4 = (bf16[512,256]{1,0:T(8,128)(2,1)S(1)}, bf16[512,256]{1,0:T(8,128)(2,1)}, u32[]{:S(2)}) copy-start(bf16[512,256]{1,0:T(8,128)(2,1)} %param.12) | copy-start | bytes 786436
  1023.7 60.0 %copy-start.5 = (f32[16,1024]{1,0:T(8,128)S(1)}, f32[16,1024]{1,0:T(8,128)}, u32[]{:S(2)}) copy-start(f32[16,1024]{1,0:T(8,128)} %param.10) | copy-start | bytes 196612
  1023.8 60.0 %copy-start.6 = (f32[512]{0:T(512)S(1)}, f32[512]{0:T(512)}, u32[]{:S(2)}) copy-start(f32[512]{0:T(512)} %param.15) | copy-start | bytes 6148
  1023.8 60.0 %copy-start.7 = (f32[512]{0:T(512)S(1)}, f32[512]{0:T(512)}, u32[]{:S(2)}) copy-start(f32[512]{0:T(512)} %param.14) | copy-start | bytes 6148
where the time goes:
time: 1320 us
  blocking collectives  949 us (72%)
  other arithmetic  140 us (11%)
  local copies, waits for them, and re-layouts  132 us (10%)
  matrix products  82.8 us (6%)
    all_to_all x1, blocking collectives, body(): lax.all_to_all(joined, 'mode', split_axis=1, concat_axis=0, tiled=True)  733 us
    all_to_all x1, blocking collectives, body(): lax.all_to_all(result, 'mode', split_axis=0, concat_axis=1, tiled=True)  188 us
    dot_general x1, matrix products, finish(): jnp.einsum('kij,kjxy->ixy', kl_modes, images, preferred_element_type=jnp....  59.9 us
    mul x2, other arithmetic, conduct(): total = total + 0.5 * (kcentre + kother) * (centre - other)  55.6 us
    convert_element_type x1, other arithmetic, conduct(): return total.astype(jnp.bfloat16)  46.6 us
    slice x2, local copies, waits for them, and re-layouts, body(): node_images = moved[1:]  42.7 us
    all_to_all x1, local copies, waits for them, and re-layouts, body(): lax.all_to_all(joined, 'mode', split_axis=1, concat_axis=0, tiled=True)  30.8 us
    all_gather x1, blocking collectives, body(): kap_rows = lax.all_gather(kappa, 'mode', axis=1, tiled=True)  28.1 us
  transfers between devices with their start and end apart: 2, of which 0 were waited for; matrix products, arithmetic and copies ran while one was open for 1% of the time, Pallas kernels for 0%

commit v1 on v0

--- a/solution.py
+++ b/solution.py
@@ -1,7 +1,40 @@
+import functools
 import jax
 import jax.numpy as jnp
 from jax import lax
 from jax.sharding import PartitionSpec as P
+from jax.lax import axis_index, axis_size, ppermute
+
+
+def arrays_derive(x_local, dim_no, frame):
+    piece_out = x_local.shape
+    return jnp.moveaxis(
+        x_local.reshape(
+            *piece_out[:dim_no], frame, piece_out[dim_no] // frame, *piece_out[dim_no + 1 :]
+        ),
+        dim_no,
+        0,
+    )
+
+
+def _part_trails(mat, d0):
+    mat = jnp.moveaxis(mat, 0, d0)
+    found_now = mat.shape
+    return mat.reshape(*found_now[:d0], found_now[d0] * found_now[d0 + 1], *found_now[d0 + 2 :])
+
+
+def define_targets_in(in_array, link_axis, chunk, packet):
+    built, h_now = (axis_size(link_axis), axis_index(link_axis))
+    a_now = arrays_derive(in_array, chunk, built)
+    queue = [a_now[h_now]]
+    for p in range(1, built):
+        mixed_arr = a_now[h_now ^ p]
+        queue.append(ppermute(mixed_arr, link_axis, [(dev_i, dev_i ^ p) for dev_i in range(built)]))
+    a_now = jnp.stack(queue, axis=0)[h_now ^ jnp.arange(built)]
+    return _part_trails(a_now, packet)
+
+
+refer_the_grid = functools.partial(define_targets_in, link_axis="mode", chunk=1, packet=0)
 
 
 def extended(cells, sides, width):
@@ -58,7 +91,7 @@
     images = conduct(padded[:owned], padded[owned:])
     joined = jnp.concatenate([coarse[None], images], 0)
     joined = joined.reshape((terms + 1) * owned, coarse.shape[1], width)
-    moved = lax.all_to_all(joined, "mode", split_axis=1, concat_axis=0, tiled=True)
+    moved = refer_the_grid(joined)
     node_rows = moved.shape[1]
     moved = moved.reshape(groups, terms + 1, owned, node_rows, width)
     moved = jnp.transpose(moved, (1, 0, 2, 3, 4)).reshape(

time: 1320 us -> 1470 us (1.11)
  blocking collectives: 949 us -> 385 us
  waiting for transfers between devices: 0.01 us -> 513 us
  local copies, waits for them, and re-layouts: 132 us -> 309 us
    all_to_all x1 -> x0, blocking collectives: 733 us -> none  [body(): lax.all_to_all(joined, 'mode', split_axis=1, concat_axis=0, tiled=True)]
    ppermute x0 -> x7, waiting for transfers between devices: none -> 513 us  [define_targets_in(): ppermute(mixed_arr, link_axis, [(dev_i, dev_i ^ p) for dev_i in range(bui...]
    all_to_all x1, blocking collectives: 188 us -> 357 us  [body(): lax.all_to_all(result, 'mode', split_axis=0, concat_axis=1, tiled=True)]
    mul x0 -> x8, local copies, waits for them, and re-layouts: none -> 79.2 us  [conduct(): total = total + 0.5 * (kcentre + kother) * (centre - other)]
    gather x0 -> x5, local copies, waits for them, and re-layouts: none -> 56.9 us  [define_targets_in(): a_now = jnp.stack(queue, axis=0)[h_now ^ jnp.arange(built)]]
    unnamed x34 -> x55, local copies, waits for them, and re-layouts: 28 us -> 63.3 us
    all_to_all x1 -> x0, local copies, waits for them, and re-layouts: 30.8 us -> none  [body(): lax.all_to_all(joined, 'mode', split_axis=1, concat_axis=0, tiled=True)]
    unnamed x2 -> x5, other arithmetic: 0.01 us -> 22.8 us
  transfers between devices with their start and end apart: 2 -> 9, of which waited for: 0 -> 4; matrix products, arithmetic and copies ran while one was open for 1% -> 4% of each run, Pallas kernels for 0% -> 0%
where the time goes in v1:
time: 1470 us; the launch traced here: 1460 us
  waiting for transfers between devices  513 us (35%)
  blocking collectives  385 us (26%)
  local copies, waits for them, and re-layouts  309 us (21%)
  other arithmetic  150 us (10%)
  matrix products  82.7 us (6%)
  starting transfers between devices  19.8 us (1%)
    ppermute x7, waiting for transfers between devices, define_targets_in(): ppermute(mixed_arr, link_axis, [(dev_i, dev_i ^ p) for dev_i in range(bui...  513 us
    all_to_all x1, blocking collectives, body(): lax.all_to_all(result, 'mode', split_axis=0, concat_axis=1, tiled=True)  357 us
    mul x8, local copies, waits for them, and re-layouts, conduct(): total = total + 0.5 * (kcentre + kother) * (centre - other)  79.2 us
    unnamed x55, local copies, waits for them, and re-layouts  63.3 us
    dot_general x1, matrix products, finish(): jnp.einsum('kij,kjxy->ixy', kl_modes, images, preferred_element_type=jnp....  59.9 us
    gather x5, local copies, waits for them, and re-layouts, define_targets_in(): a_now = jnp.stack(queue, axis=0)[h_now ^ jnp.arange(built)]  56.9 us
    mul x2, other arithmetic, conduct(): total = total + 0.5 * (kcentre + kother) * (centre - other)  56.5 us
    slice x2, local copies, waits for them, and re-layouts, body(): node_images = moved[1:]  42.7 us
  transfers between devices with their start and end apart: 9, of which 4 were waited for; matrix products, arithmetic and copies ran while one was open for 4% of the time, Pallas kernels for 0%

profile of v1, /device:TPU:1, one launch (start us, length us, event | category | flops | bytes accessed | tf_op | source)
XLA Modules:
  0.0 1460.7 jit_solution(12161880497226152419)
XLA Ops:
  0.0 0.0 slice-start.8
  0.0 16.5 %copy.64 = bf16[32,128,1024]{2,0,1:T(8,128)(2,1)S(1)} copy(f32[32,128,1024]{2,1,0:T(8,128)} %param.8) | data formatting | bytes 25165824 | tf_op args[0]
  16.6 0.0 copy-start.1
  16.6 28.1 %all_gather.3 = bf16[3,128,1024]{2,1,0:T(8,128)(2,1)S(1)} all-gather(bf16[3,16,1024]{2,1,0:T(8,128)(2,1)S(1)} %copy-done.3), channel_id=1, replica_groups=mesh['mesh'=4,'mode'=8] {'mode'}, dimensions={1}, use_global_device_ids=true | all-gather | bytes 884736 | tf_op jit(solution)/shard_map/all_gather | solution.py:88
  44.6 0.7 copy.37
  45.3 0.0 slice-start.9
  45.4 9.1 collective-permute-start
  54.5 2.1 collective-permute-start.1
  56.7 11.4 copy.66
  68.1 11.4 copy.46
  79.5 0.0 collective-permute-done.1
  79.5 14.2 fusion.11
  93.7 51.8 %fusion.6 = (f32[32,128,1024]{2,0,1:T(8,128)}, f32[32,128,1024]{2,0,1:T(8,128)}, f32[32,128,1024]{2,0,1:T(8,128)}, f32[32,128,1024]{2,0,1:T(8,128)}) fusion(f32[1,32,130,1026]{3,1,2,0:T(8,128)} %fusion.11), kind=kLoop, calls=%fused_computation.19 | loop fusion | flops 16777216 | bytes 150994944 | tf_op jit(solution)/shard_map/mul | solution.py:68
  145.5 19.1 %copy.39 = f32[32,128,1024]{2,1,0:T(8,128)} copy(f32[32,128,1024]{2,0,1:T(8,128)} %get-tuple-element.14) | data formatting | bytes 33554432 | tf_op jit(solution)/shard_map/mul | solution.py:68
  164.7 19.0 %copy.41 = f32[32,128,1024]{2,1,0:T(8,128)} copy(f32[32,128,1024]{2,0,1:T(8,128)S(1)} %copy-done.2) | data formatting | bytes 33554432 | tf_op jit(solution)/shard_map/mul | solution.py:68
  183.7 18.3 %copy.43 = f32[32,128,1024]{2,1,0:T(8,128)} copy(f32[32,128,1024]{2,0,1:T(8,128)} %get-tuple-element.15) | data formatting | bytes 33554432 | tf_op jit(solution)/shard_map/mul | solution.py:68
  202.0 19.1 %copy.45 = f32[32,128,1024]{2,1,0:T(8,128)} copy(f32[32,128,1024]{2,0,1:T(8,128)S(1)} %bitcast.104) | data formatting | bytes 33554432 | tf_op jit(solution)/shard_map/mul | solution.py:68
  221.1 2.8 fusion.38
  223.9 0.0 slice-start.10
  224.0 0.0 slice-start.11
  224.0 4.7 fusion.36
  228.7 0.9 copy.38
  229.6 0.0 slice-start.13
  229.7 0.9 copy.40
  230.6 0.9 copy.42
  231.5 0.9 copy.44
  232.5 30.4 %add_convert_fusion = bf16[3,32,128,1024]{3,2,1,0:T(8,128)(2,1)} fusion(f32[32,128,1024]{2,1,0:T(8,128)} %copy.45, f32[3,128,1024]{2,1,0:T(8,128)S(1)} %copy.44, f32[32,128,1024]{2,1,0:T(8,128)} %copy.43, f32[3,128,1024]{2,1,0:T(8,128)S(1)} %copy.42, f32[32,128,1024]{2,1,0:T(8,128)} %copy.41, f32[3,128,1024]{2,1,0:T(8,128)S(1)} %copy.40, ...), kind=kLoop, calls=%fused_computation.3 | loop fusion | flops 100663296 | bytes 98566144 | tf_op jit(solution)/shard_map/convert_element_type | solution.py:69
  262.9 23.1 %pad_maximum_fusion = bf16[4,32,128,1024]{3,2,1,0:T(8,128)(2,1)} fusion(bf16[3,32,128,1024]{3,2,1,0:T(8,128)(2,1)} %add_convert_fusion, bf16[1,32,128,1024]{3,2,1,0:T(8,128)(2,1)} %copy.46), kind=kLoop, calls=%fused_computation.4 | loop fusion | flops 16777216 | bytes 67108864 | tf_op jit(solution)/shard_map/concatenate | solution.py:92
  286.0 20.6 %dynamic-slice_bitcast_fusion = (bf16[128,16,1024]{2,1,0:T(8,128)(2,1)}, bf16[128,16,1024]{2,1,0:T(8,128)(2,1)}, bf16[128,16,1024]{2,1,0:T(8,128)(2,1)}, bf16[12...) fusion(bf16[128,8,16,1024]{3,2,1,0:T(8,128)(2,1)} %bitcast.101,, ...), kind=kLoop, calls=%fused_computation.43 | loop fusion | bytes 58720284 | tf_op jit(solution)/shard_map/squeeze | solution.py:31
  306.6 1.3 collective-permute-start.2
  307.9 0.0 collective-permute-start.3
  307.9 1.4 collective-permute-start.4
  309.3 1.9 collective-permute-start.5
  311.2 1.5 collective-permute-start.6
  312.7 85.0 %collective-permute-done.2 = bf16[128,16,1024]{2,1,0:T(8,128)(2,1)} collective-permute-done((bf16[128,16,1024]{2,1,0:T(8,128)(2,1)}, bf16[128,16,1024]{2,1,0:T(8,128)(2,1)}, u32[]{:S(2)}, u32[]{:S(2)}) %collective-permute-start.2) | collective-permute-done | bytes 4194336 | tf_op jit(solution)/shard_map/ppermute | solution.py:32
  397.7 2.5 collective-permute-start.7
  400.2 178.9 %collective-permute-done.3 = bf16[128,16,1024]{2,1,0:T(8,128)(2,1)} collective-permute-done((bf16[128,16,1024]{2,1,0:T(8,128)(2,1)}, bf16[128,16,1024]{2,1,0:T(8,128)(2,1)}, u32[]{:S(2)}, u32[]{:S(2)}) %collective-permute-start.3) | collective-permute-done | bytes 4194336 | tf_op jit(solution)/shard_map/ppermute | solution.py:32
  579.1 5.1 bitcast_dynamic-update-slice_fusion.7
  584.3 5.0 bitcast_dynamic-update-slice_fusion.6
  589.3 5.0 bitcast_dynamic-update-slice_fusion.5
  594.3 71.5 %collective-permute-done.4 = bf16[128,16,1024]{2,1,0:T(8,128)(2,1)} collective-permute-done((bf16[128,16,1024]{2,1,0:T(8,128)(2,1)}, bf16[128,16,1024]{2,1,0:T(8,128)(2,1)}, u32[]{:S(2)}, u32[]{:S(2)}) %collective-permute-start.4) | collective-permute-done | bytes 4194336 | tf_op jit(solution)/shard_map/ppermute | solution.py:32
  665.8 5.0 bitcast_dynamic-update-slice_fusion.4
  670.8 5.1 bitcast_dynamic-update-slice_fusion.3
  675.9 177.4 %collective-permute-done.6 = bf16[128,16,1024]{2,1,0:T(8,128)(2,1)} collective-permute-done((bf16[128,16,1024]{2,1,0:T(8,128)(2,1)}, bf16[128,16,1024]{2,1,0:T(8,128)(2,1)}, u32[]{:S(2)}, u32[]{:S(2)}) %collective-permute-start.6) | collective-permute-done | bytes 4194336 | tf_op jit(solution)/shard_map/ppermute | solution.py:32
  853.2 5.0 bitcast_dynamic-update-slice_fusion.2
  858.3 5.0 bitcast_dynamic-update-slice_fusion.1
  863.3 5.0 bitcast_dynamic-update-slice_fusion
  868.3 18.8 %fusion.49 = (bf16[8,128,16,384]{3,2,1,0:T(8,128)(2,1)}, bf16[8,128,16,384]{3,2,1,0:T(8,128)(2,1)}) fusion(bf16[8,128,16,1024]{3,2,1,0:T(8,128)(2,1)} %bitcast_dynamic-update-slice_fusion), kind=kLoop, calls=%fused_computation.82 | loop fusion | bytes 50331648 | tf_op jit(solution)/shard_map/gather | solution.py:33
  887.0 7.3 mini-gather-slice.5
  894.4 11.4 gather_fusion
  905.7 11.4 gather_fusion.1
  917.1 8.1 gather_fusion.2
  925.2 22.8 %pad_maximum_fusion.1 = bf16[8,128,16,1024]{3,2,1,0:T(8,128)(2,1)} fusion(bf16[8,128,16,256]{3,2,1,0:T(8,128)(2,1)} %gather_fusion.2, bf16[8,128,16,384]{3,2,1,0:T(8,128)(2,1)} %gather_fusion.1, bf16[8,128,16,384]{3,2,1,0:T(8,128)(2,1)} %gather_fusion), kind=kLoop, calls=%fused_computation.5 | loop fusion | flops 100663296 | bytes 67108864
  948.0 21.3 %slice.86 = bf16[3,8,32,16,1024]{4,3,2,0,1:T(8,128)(2,1)} slice(bf16[4,8,32,16,1024]{4,3,2,0,1:T(8,128)(2,1)} %bitcast.99), slice={[1:4], [0:8], [0:32], [0:16], [0:1024]} | slice | bytes 50331648 | tf_op jit(solution)/shard_map/slice | solution.py:101
  969.3 8.7 slice.85
  978.0 21.4 %copy.48 = bf16[3,8,32,16,1024]{4,3,2,1,0:T(8,128)(2,1)} copy(bf16[3,8,32,16,1024]{4,3,2,0,1:T(8,128)(2,1)} %slice.86) | data formatting | bytes 50331648 | tf_op jit(solution)/shard_map/slice | solution.py:101
  999.4 0.0 copy-start.6
  999.4 0.0 copy-start.7
  999.4 0.0 copy-start.8
  999.4 59.9 %fusion = f32[16,1024,256,1]{2,1,3,0:T(8,128)} fusion(bf16[3,256,16,1024]{3,2,1,0:T(8,128)(2,1)} %bitcast.111, bf16[3,256,256]{2,1,0:T(8,128)(2,1)S(1)} %copy-done), kind=kOutput, calls=%fused_computation.9 | convolution fusion | flops 6442450944 | bytes 42336256 | tf_op jit(solution)/shard_map/kij,kjxy->ixy/dot_general | solution.py:73
  1059.4 22.9 %fusion.23 = bf16[256,16,1024]{0,2,1:T(8,128)(2,1)} fusion(f32[16,1024,256,1]{2,1,3,0:T(8,128)} %fusion, f32[512]{0:T(512)S(1)} %copy-done.7, f32[512]{0:T(512)S(1)} %copy-done.8, bf16[256,16,1024]{2,1,0:T(8,128)(2,1)} %bitcast.112, f32[16,1024]{1,0:T(8,128)S(1)} %copy-done.6, bf16[256,512]{1,0:T(8,128)(2,1)S(1)} %copy-done.4, ...), kind=kOutput, calls=%fused_computation.34 | convolution fusion | flops 8669626368 | bytes 34148352 | tf_op jit(solution)/shard_map/iq,qxy->ixy/dot_general | solution.py:78
  1082.2 12.2 copy.50
  1094.5 357.2 %all_to_all.18 = bf16[256,16,1024]{2,1,0:T(8,128)(2,1)} all-to-all(bf16[256,16,1024]{2,1,0:T(8,128)(2,1)} %copy.50), channel_id=1, replica_groups=mesh['mesh'=4,'mode'=8] {'mode'}, dimensions={0} | all-to-all | bytes 16777216 | tf_op jit(solution)/shard_map/all_to_all | solution.py:105
  1451.6 8.7 copy.51
  (49 shorter events, 0.1 us)
Async XLA Ops:
  0.0 999.4 %copy-start = (bf16[3,256,256]{2,1,0:T(8,128)(2,1)S(1)}, bf16[3,256,256]{2,1,0:T(8,128)(2,1)}, u32[]{:S(2)}) copy-start(bf16[3,256,256]{2,1,0:T(8,128)(2,1)} %param.11) | copy-start | bytes 1179652
  0.0 56.6 %slice-start.6 = ((s8[16777216]{0:T(1024)(128)(4,1)}), s8[4194304]{0:T(1024)(128)(4,1)S(1)}, s32[]{:S(2)}) async-start(s8[16777216]{0:T(1024)(128)(4,1)} %bitcast.105), calls=%async_computation.7 | async-start | bytes 8388608
  0.0 56.7 %slice-start.7 = ((s8[16777216]{0:T(1024)(128)(4,1)}), s8[4194304]{0:T(1024)(128)(4,1)S(1)}, s32[]{:S(2)}) async-start(s8[16777216]{0:T(1024)(128)(4,1)} %bitcast.105), calls=%async_computation.8 | async-start | bytes 8388608
  0.0 56.7 %slice-start.8 = ((s8[16777216]{0:T(1024)(128)(4,1)}), s8[4194304]{0:T(1024)(128)(4,1)S(1)}, s32[]{:S(2)}) async-start(s8[16777216]{0:T(1024)(128)(4,1)} %bitcast.105), calls=%async_computation.9 | async-start | bytes 8388608
  0.0 16.6 %copy-start.3 = (bf16[3,16,1024]{2,1,0:T(8,128)(2,1)S(1)}, bf16[3,16,1024]{2,1,0:T(8,128)(2,1)}, u32[]{:S(2)}) copy-start(bf16[3,16,1024]{2,1,0:T(8,128)(2,1)} %param.9) | copy-start | bytes 294916
  16.6 51.5 %copy-start.1 = (bf16[32,128,1024]{2,0,1:T(8,128)(2,1)}, bf16[32,128,1024]{2,0,1:T(8,128)(2,1)S(1)}, u32[]{:S(2)}) copy-start(bf16[32,128,1024]{2,0,1:T(8,128)(2,1)S(1)} %copy.64) | copy-start | bytes 25165828
  45.3 11.3 slice-start.9
  45.4 34.2 %collective-permute-start = (bf16[35,1,1024]{2,0,1:T(8,128)(2,1)S(1)}, bf16[35,1,1024]{2,0,1:T(8,128)(2,1)S(1)}, u32[]{:S(2)}, u32[]{:S(2)}) collective-permute-start(bf16[35,1,1024]{2,0,1:T(8,128)(2,1)S(1)} %get-tuple-element.18), channel_id=1, source_target_pairs={{0,8},{8,16},{16,24},{1,9},{9,17},{17,25},{2,10},{10,18},{18,26},{... | collective-permute-start | bytes 215048 | tf_op jit(solution)/shard_map/ppermute | solution.py:48
  54.5 25.0 %collective-permute-start.1 = (bf16[35,1,1024]{2,0,1:T(8,128)(2,1)S(1)}, bf16[35,1,1024]{2,0,1:T(8,128)(2,1)S(1)}, u32[]{:S(2)}, u32[]{:S(2)}) collective-permute-start(bf16[35,1,1024]{2,0,1:T(8,128)(2,1)S(1)} %get-tuple-element.19), channel_id=1, source_target_pairs={{8,0},{16,8},{24,16},{9,1},{17,9},{25,17},{10,2},{18,10},{26,18},{... | collective-permute-start | bytes 215048 | tf_op jit(solution)/shard_map/ppermute | solution.py:50
  145.5 19.1 %copy-start.2 = (f32[32,128,1024]{2,0,1:T(8,128)S(1)}, f32[32,128,1024]{2,0,1:T(8,128)}, u32[]{:S(2)}) copy-start(f32[32,128,1024]{2,0,1:T(8,128)} %get-tuple-element.16) | copy-start | bytes 50331652
  164.7 37.3 %slice-start.2 = ((s8[16777216]{0:T(1024)(128)(4,1)}), s8[4194304]{0:T(1024)(128)(4,1)S(1)}, s32[]{:S(2)}) async-start(s8[16777216]{0:T(1024)(128)(4,1)} %bitcast.103), calls=%async_computation.3 | async-start | bytes 8388608
  164.7 37.3 %slice-start.3 = ((s8[16777216]{0:T(1024)(128)(4,1)}), s8[4194304]{0:T(1024)(128)(4,1)S(1)}, s32[]{:S(2)}) async-start(s8[16777216]{0:T(1024)(128)(4,1)} %bitcast.103), calls=%async_computation.4 | async-start | bytes 8388608
  183.7 18.3 %slice-start.4 = ((s8[16777216]{0:T(1024)(128)(4,1)}), s8[4194304]{0:T(1024)(128)(4,1)S(1)}, s32[]{:S(2)}) async-start(s8[16777216]{0:T(1024)(128)(4,1)} %bitcast.103), calls=%async_computation.5 | async-start | bytes 8388608
  183.7 18.3 %slice-start.5 = ((s8[16777216]{0:T(1024)(128)(4,1)}), s8[4194304]{0:T(1024)(128)(4,1)S(1)}, s32[]{:S(2)}) async-start(s8[16777216]{0:T(1024)(128)(4,1)} %bitcast.103), calls=%async_computation.6 | async-start | bytes 8388608
  183.7 37.4 %slice-start = ((s8[8388608]{0:T(1024)(128)(4,1)}), s8[4194304]{0:T(1024)(128)(4,1)S(1)}, s32[]{:S(2)}) async-start(s8[8388608]{0:T(1024)(128)(4,1)} %bitcast.97), calls=%async_computation.1 | async-start | bytes 8388608
  202.0 19.1 %slice-start.1 = ((s8[8388608]{0:T(1024)(128)(4,1)}), s8[4194304]{0:T(1024)(128)(4,1)S(1)}, s32[]{:S(2)}) async-start(s8[8388608]{0:T(1024)(128)(4,1)} %bitcast.97), calls=%async_computation.2 | async-start | bytes 8388608
  223.9 8.5 slice-start.10
  224.0 8.5 slice-start.11
  224.0 8.5 slice-start.12
  229.6 2.8 slice-start.13
  306.6 91.1 %collective-permute-start.2 = (bf16[128,16,1024]{2,1,0:T(8,128)(2,1)}, bf16[128,16,1024]{2,1,0:T(8,128)(2,1)}, u32[]{:S(2)}, u32[]{:S(2)}) collective-permute-start(bf16[128,16,1024]{2,1,0:T(8,128)(2,1)} %get-tuple-element.13), channel_id=1, source_target_pairs={{0,1},{1,0},{2,3},{3,2},{4,5},{5,4},{6,7},{7,6},{8,9},{9,8},{10,11... | collective-permute-start | bytes 12582920 | tf_op jit(solution)/shard_map/ppermute | solution.py:32
  307.9 271.2 %collective-permute-start.3 = (bf16[128,16,1024]{2,1,0:T(8,128)(2,1)}, bf16[128,16,1024]{2,1,0:T(8,128)(2,1)}, u32[]{:S(2)}, u32[]{:S(2)}) collective-permute-start(bf16[128,16,1024]{2,1,0:T(8,128)(2,1)} %get-tuple-element.12), channel_id=1, source_target_pairs={{0,2},{1,3},{2,0},{3,1},{4,6},{5,7},{6,4},{7,5},{8,10},{9,11},{10,... | collective-permute-start | bytes 12582920 | tf_op jit(solution)/shard_map/ppermute | solution.py:32
  307.9 357.8 %collective-permute-start.4 = (bf16[128,16,1024]{2,1,0:T(8,128)(2,1)}, bf16[128,16,1024]{2,1,0:T(8,128)(2,1)}, u32[]{:S(2)}, u32[]{:S(2)}) collective-permute-start(bf16[128,16,1024]{2,1,0:T(8,128)(2,1)} %get-tuple-element.11), channel_id=1, source_target_pairs={{0,3},{1,2},{2,1},{3,0},{4,7},{5,6},{6,5},{7,4},{8,11},{9,10},{10,... | collective-permute-start | bytes 12582920 | tf_op jit(solution)/shard_map/ppermute | solution.py:32
  309.3 361.5 %collective-permute-start.5 = (bf16[128,16,1024]{2,1,0:T(8,128)(2,1)}, bf16[128,16,1024]{2,1,0:T(8,128)(2,1)}, u32[]{:S(2)}, u32[]{:S(2)}) collective-permute-start(bf16[128,16,1024]{2,1,0:T(8,128)(2,1)} %get-tuple-element.10), channel_id=1, source_target_pairs={{0,4},{1,5},{2,6},{3,7},{4,0},{5,1},{6,2},{7,3},{8,12},{9,13},{10,... | collective-permute-start | bytes 12582920 | tf_op jit(solution)/shard_map/ppermute | solution.py:32
  311.2 542.0 %collective-permute-start.6 = (bf16[128,16,1024]{2,1,0:T(8,128)(2,1)}, bf16[128,16,1024]{2,1,0:T(8,128)(2,1)}, u32[]{:S(2)}, u32[]{:S(2)}) collective-permute-start(bf16[128,16,1024]{2,1,0:T(8,128)(2,1)} %get-tuple-element.9), channel_id=1, source_target_pairs={{0,5},{1,4},{2,7},{3,6},{4,1},{5,0},{6,3},{7,2},{8,13},{9,12},{10,... | collective-permute-start | bytes 12582920 | tf_op jit(solution)/shard_map/ppermute | solution.py:32
  397.7 460.6 %collective-permute-start.7 = (bf16[128,16,1024]{2,1,0:T(8,128)(2,1)}, bf16[128,16,1024]{2,1,0:T(8,128)(2,1)}, u32[]{:S(2)}, u32[]{:S(2)}) collective-permute-start(bf16[128,16,1024]{2,1,0:T(8,128)(2,1)} %get-tuple-element.8), channel_id=1, source_target_pairs={{0,6},{1,7},{2,4},{3,5},{4,2},{5,3},{6,0},{7,1},{8,14},{9,15},{10,... | collective-permute-start | bytes 12582920 | tf_op jit(solution)/shard_map/ppermute | solution.py:32
  579.1 284.2 %collective-permute-start.8 = (bf16[128,16,1024]{2,1,0:T(8,128)(2,1)}, bf16[128,16,1024]{2,1,0:T(8,128)(2,1)}, u32[]{:S(2)}, u32[]{:S(2)}) collective-permute-start(bf16[128,16,1024]{2,1,0:T(8,128)(2,1)} %get-tuple-element.7), channel_id=1, source_target_pairs={{0,7},{1,6},{2,5},{3,4},{4,3},{5,2},{6,1},{7,0},{8,15},{9,14},{10,... | collective-permute-start | bytes 12582920 | tf_op jit(solution)/shard_map/ppermute | solution.py:32
  999.4 59.9 %copy-start.4 = (bf16[256,512]{1,0:T(8,128)(2,1)S(1)}, bf16[256,512]{1,0:T(8,128)(2,1)}, u32[]{:S(2)}) copy-start(bf16[256,512]{1,0:T(8,128)(2,1)} %param.13) | copy-start | bytes 786436
  999.4 59.9 %copy-start.5 = (bf16[512,256]{1,0:T(8,128)(2,1)S(1)}, bf16[512,256]{1,0:T(8,128)(2,1)}, u32[]{:S(2)}) copy-start(bf16[512,256]{1,0:T(8,128)(2,1)} %param.12) | copy-start | bytes 786436
  999.4 59.9 %copy-start.6 = (f32[16,1024]{1,0:T(8,128)S(1)}, f32[16,1024]{1,0:T(8,128)}, u32[]{:S(2)}) copy-start(f32[16,1024]{1,0:T(8,128)} %param.10) | copy-start | bytes 196612
  999.4 59.9 %copy-start.7 = (f32[512]{0:T(512)S(1)}, f32[512]{0:T(512)}, u32[]{:S(2)}) copy-start(f32[512]{0:T(512)} %param.15) | copy-start | bytes 6148
  999.4 59.9 %copy-start.8 = (f32[512]{0:T(512)S(1)}, f32[512]{0:T(512)}, u32[]{:S(2)}) copy-start(f32[512]{0:T(512)} %param.14) | copy-start | bytes 6148
